TPU v7x, 32 devices: a whole 2x2x4 slice. The times are simulated.
32 devices in a mesh: section: 4 (over y, x), expert: 8 (over z, core).
Axes of the slice: x: 2, y: 2, z: 4, core: 2. Of those that a mesh axis runs over, the one named last changes fastest.
Arguments:
- forward_held: bfloat16 [4, 512, 3584], P('section', 'expert'), may hold values from -6 to 6
- forward_enter: bfloat16 [1, 512, 3584], P(None, 'expert'), may hold values from -6 to 6
- backward_held: bfloat16 [4, 512, 3584], P('section', 'expert'), may hold values from -6 to 6
- backward_enter: bfloat16 [1, 512, 3584], P(None, 'expert'), may hold values from -6 to 6
- stashed_inputs: bfloat16 [4, 2, 512, 3584], P('section', None, 'expert'), may hold values from -6 to 6
- gate_weight: bfloat16 [4, 16, 3584, 1024], P('section', 'expert'), may hold values from -0.09375 to 0.09375
- up_weight: bfloat16 [4, 16, 3584, 1024], P('section', 'expert'), may hold values from -0.09375 to 0.09375
- down_weight: bfloat16 [4, 16, 1024, 3584], P('section', 'expert'), may hold values from -0.1875 to 0.1875
- norm_gain: float32 [4, 3584], P('section'), may hold values from 0.5 to 2
- expert_ids: int32 [4, 4, 512, 2], P('section', None, 'expert'), may hold values from 0 to 15, all different within a row; in each aligned block of 64 rows (0 to 63, 64 to 127, ..., all dimensions but the last counted through in order) at most 12 rows name the same one
- router_scores: float32 [4, 4, 512, 2], P('section', None, 'expert'), may hold values from 0.02 to 1
Outputs:
- forward_out: bfloat16 [2, 4, 512, 3584], P(None, 'section', 'expert')
- backward_out: bfloat16 [2, 4, 512, 3584], P(None, 'section', 'expert')
Inputs may be any that keep to these rules, and one draw needn't show every extreme that they name: `expert_ids`: each token names 2 different experts; in each section, micro-batch index and aligned block of 64 tokens no expert is named by more than 12 tokens.
All inputs are finite; a program needn't handle non-finite values.
Results may differ from a plain program's by a relative error of at most 0.0087.
Values may be sent and summed in bfloat16 or wider, within the bound.
A program may use at most 192 MiB of HBM per device.

v0:
```python
import jax
import jax.numpy as jnp
from jax import lax
from jax.sharding import PartitionSpec as P

EXPERTS = 16
TOPK = 2
TICKS = 2
CAP = 12


EPSILON = 1e-06
ROUTE_SCALE = 2.5


def passed_along(value, axis, steps):
    count = lax.axis_size(axis)
    leading, last = (max(0, -steps), min(count, count - steps))
    return lax.ppermute(value, axis, [(source, source + steps) for source in range(leading, last)])


def normalized(values, gain):
    floats = values.astype(jnp.float32)
    inverse = lax.rsqrt(jnp.mean(floats * floats, axis=-1, keepdims=True) + EPSILON)
    return (floats, inverse, (floats * inverse * gain).astype(jnp.bfloat16))


def gate_values(scores):
    return ROUTE_SCALE * scores / jnp.sum(scores, axis=-1, keepdims=True)


def slot_table(chosen_ids, capacity, experts):
    flat = chosen_ids.reshape(-1)
    onehot = (flat[:, None] == jnp.arange(experts, dtype=jnp.int32)[None, :]).astype(jnp.int32)
    earlier = jnp.cumsum(onehot, axis=0) - onehot
    place = jnp.sum(earlier * onehot, axis=1)
    return flat * capacity + place


def slot_selector(slots, total_slots):
    return (slots[:, None] == jnp.arange(total_slots, dtype=jnp.int32)[None, :]).astype(
        jnp.bfloat16
    )


def expert_forward(received, gate_local, up_local, down_local, groups):
    local_count = gate_local.shape[0]
    items = received.shape[1]
    width = received.shape[2]
    blocks = received.reshape(groups, local_count, items, width)
    pre_gate = jnp.einsum("sejd,edf->sejf", blocks, gate_local, preferred_element_type=jnp.float32)
    pre_up = jnp.einsum("sejd,edf->sejf", blocks, up_local, preferred_element_type=jnp.float32)
    active = (jax.nn.silu(pre_gate) * pre_up).astype(jnp.bfloat16)
    result = jnp.einsum(
        "sejf,efd->sejd", active, down_local, preferred_element_type=jnp.float32
    ).astype(jnp.bfloat16)
    return result.reshape(groups * local_count, items, width)


def expert_backward(received_normed, received_grad, gate_local, up_local, down_local, groups):
    local_count = gate_local.shape[0]
    items = received_normed.shape[1]
    width = received_normed.shape[2]
    blocks = received_normed.reshape(groups, local_count, items, width)
    grad_blocks = received_grad.reshape(groups, local_count, items, width)
    pre_gate = jnp.einsum("sejd,edf->sejf", blocks, gate_local, preferred_element_type=jnp.float32)
    pre_up = jnp.einsum("sejd,edf->sejf", blocks, up_local, preferred_element_type=jnp.float32)
    sigma = jax.nn.sigmoid(pre_gate)
    swish = pre_gate * sigma
    act_grad = jnp.einsum(
        "sejd,efd->sejf", grad_blocks, down_local, preferred_element_type=jnp.float32
    )
    d_gate = (act_grad * pre_up * sigma * (1.0 + pre_gate * (1.0 - sigma))).astype(jnp.bfloat16)
    d_up = (act_grad * swish).astype(jnp.bfloat16)
    normed_grad = jnp.einsum(
        "sejf,edf->sejd", d_gate, gate_local, preferred_element_type=jnp.float32
    ) + jnp.einsum("sejf,edf->sejd", d_up, up_local, preferred_element_type=jnp.float32)
    return normed_grad.astype(jnp.bfloat16).reshape(groups * local_count, items, width)


def local(
    forward_held,
    forward_enter,
    backward_held,
    backward_enter,
    stashed_inputs,
    gate_weight,
    up_weight,
    down_weight,
    norm_gain,
    expert_ids,
    router_scores,
):
    position = lax.axis_index("section")
    sections = lax.axis_size("section")
    groups = lax.axis_size("expert")
    gate_local = gate_weight[0]
    up_local = up_weight[0]
    down_local = down_weight[0]
    gain = norm_gain[0]
    rows = forward_held.shape[1]
    width = forward_held.shape[2]
    total_slots = EXPERTS * CAP
    forward_rows = []
    backward_rows = []
    forward_recv = forward_held[0]
    backward_recv = backward_held[0]
    for tick_index in range(TICKS):
        if tick_index == 0:
            layer_input = forward_held[0]
            cotangent = backward_held[0]
        else:
            layer_input = jnp.where(position == 0, forward_enter[tick_index - 1], forward_recv)
            cotangent = jnp.where(
                position == sections - 1, backward_enter[tick_index - 1], backward_recv
            )
        ahead_floats, ahead_inverse, ahead_normed = normalized(layer_input, gain)
        ahead_gates = gate_values(router_scores[0, tick_index])
        ahead_slots = slot_table(expert_ids[0, tick_index], CAP, EXPERTS)
        ahead_select = slot_selector(ahead_slots, total_slots).reshape(rows, TOPK, total_slots)
        ahead_tokens = jnp.sum(ahead_select, axis=1)
        ahead_send = jnp.einsum(
            "rs,rd->sd", ahead_tokens, ahead_normed, preferred_element_type=jnp.float32
        )
        ahead_send = ahead_send.astype(jnp.bfloat16).reshape(EXPERTS, CAP, width)
        stashed = stashed_inputs[0, tick_index]
        behind_floats, behind_inverse, behind_normed = normalized(stashed, gain)
        behind_gates = gate_values(router_scores[0, TICKS + tick_index])
        behind_slots = slot_table(expert_ids[0, TICKS + tick_index], CAP, EXPERTS)
        behind_select = slot_selector(behind_slots, total_slots)
        behind_tokens = jnp.sum(behind_select.reshape(rows, TOPK, total_slots), axis=1)
        incoming = cotangent.astype(jnp.float32)
        weighted = (
            (behind_gates[..., None] * incoming[:, None, :])
            .astype(jnp.bfloat16)
            .reshape(rows * TOPK, width)
        )
        normed_send = jnp.einsum(
            "rs,rd->sd", behind_tokens, behind_normed, preferred_element_type=jnp.float32
        )
        normed_send = normed_send.astype(jnp.bfloat16).reshape(EXPERTS, CAP, width)
        grad_send = jnp.einsum(
            "ps,pd->sd", behind_select, weighted, preferred_element_type=jnp.float32
        )
        grad_send = grad_send.astype(jnp.bfloat16).reshape(EXPERTS, CAP, width)
        ahead = expert_forward(
            lax.all_to_all(ahead_send, "expert", split_axis=0, concat_axis=0, tiled=True),
            gate_local,
            up_local,
            down_local,
            groups,
        )
        behind = expert_backward(
            lax.all_to_all(normed_send, "expert", split_axis=0, concat_axis=0, tiled=True),
            lax.all_to_all(grad_send, "expert", split_axis=0, concat_axis=0, tiled=True),
            gate_local,
            up_local,
            down_local,
            groups,
        )
        ahead_back = lax.all_to_all(ahead, "expert", split_axis=0, concat_axis=0, tiled=True)
        behind_back = lax.all_to_all(behind, "expert", split_axis=0, concat_axis=0, tiled=True)
        ahead_picked = jnp.take(ahead_back.reshape(total_slots, width), ahead_slots, axis=0)
        ahead_picked = ahead_picked.reshape(rows, TOPK, width).astype(jnp.float32)
        produced = (ahead_floats + jnp.sum(ahead_gates[..., None] * ahead_picked, axis=1)).astype(
            jnp.bfloat16
        )
        behind_picked = jnp.take(behind_back.reshape(total_slots, width), behind_slots, axis=0)
        behind_picked = behind_picked.reshape(rows, TOPK, width).astype(jnp.float32)
        combined = jnp.sum(behind_picked, axis=1) * gain
        norm_term = behind_inverse * combined - behind_floats * behind_inverse**3 * jnp.mean(
            behind_floats * combined, axis=-1, keepdims=True
        )
        returned = (incoming + norm_term).astype(jnp.bfloat16)
        forward_rows.append(produced)
        backward_rows.append(returned)
        if tick_index + 1 < TICKS:
            forward_recv = passed_along(produced, "section", 1)
            backward_recv = passed_along(returned, "section", -1)
    return (jnp.stack(forward_rows)[:, None], jnp.stack(backward_rows)[:, None])


def solution(mesh):
    placed = (
        P("section", "expert", None),
        P(None, "expert", None),
        P("section", "expert", None),
        P(None, "expert", None),
        P("section", None, "expert", None),
        P("section", "expert", None, None),
        P("section", "expert", None, None),
        P("section", "expert", None, None),
        P("section", None),
        P("section", None, "expert", None),
        P("section", None, "expert", None),
    )
    return jax.shard_map(
        local,
        mesh=mesh,
        in_specs=placed,
        out_specs=(P(None, "section", "expert", None), P(None, "section", "expert", None)),
        check_vma=False,
    )
```

profile of v0, /device:TPU:0, one launch (start us, length us, event | category | flops | bytes accessed | tf_op | source)
XLA Modules:
  0.0 513.4 jit_solution(6260319966196710865)
XLA Ops:
  7.6 6.5 %all-to-all-start.5 = ((bf16[16,12,3584]{2,1,0:T(8,128)(2,1)}), bf16[16,12,3584]{2,1,0:T(8,128)(2,1)S(1)}, u32[]{:S(2)}, u32[]{:S(2)}) async-start(bf16[16,12,3584]{2,1,0:T(8,128)(2,1)} %reshape.450), calls=%async_computation.5 | async-start | bytes 3670016 | tf_op jit(solution)/shard_map/all_to_all | solution.py:154
  26.7 30.7 %all-to-all-done.5 = bf16[16,12,3584]{2,1,0:T(8,128)(2,1)S(1)} async-done(((bf16[16,12,3584]{2,1,0:T(8,128)(2,1)}), bf16[16,12,3584]{2,1,0:T(8,128)(2,1)S(1)}, u32[]{:S(2)}, u32[]{:S(2)}) %all-to-all-start.5) | async-done | bytes 1376288 | tf_op jit(solution)/shard_map/all_to_all | solution.py:154
  57.5 4.3 all-to-all-start.4
  67.9 8.2 %fusion.82 = f32[8,2,12,1024]{3,2,0,1:T(8,128)} fusion(bf16[1,2,3584,1024]{3,2,1,0:T(8,128)(2,1)} %param.18, bf16[8,2,12,3584]{3,2,1,0:T(8,128)(2,1)S(1)} %bitcast.296), kind=kOutput, calls=%fused_computation.75 | convolution fusion | flops 1409286144 | bytes 16842752 | tf_op jit(solution)/shard_map/sejd,edf->sejf/dot_general | solution.py:66
  76.1 29.1 %all-to-all-done.4 = bf16[16,12,3584]{2,1,0:T(8,128)(2,1)} async-done(((bf16[16,12,3584]{2,1,0:T(8,128)(2,1)}), bf16[16,12,3584]{2,1,0:T(8,128)(2,1)}, u32[]{:S(2)}, u32[]{:S(2)}) %all-to-all-start.4) | async-done | bytes 1376288 | tf_op jit(solution)/shard_map/all_to_all | solution.py:155
  105.2 4.5 all-to-all-start
  109.8 11.5 %fusion.112 = f32[8,2,12,1024]{3,2,0,1:T(8,128)} fusion(bf16[1,2,1024,3584]{3,2,1,0:T(8,128)(2,1)} %param.20, bf16[8,2,12,3584]{3,2,1,0:T(8,128)(2,1)} %bitcast.33), kind=kOutput, calls=%fused_computation.81 | convolution fusion | flops 1409286144 | bytes 16842752 | tf_op jit(solution)/shard_map/sejd,efd->sejf/dot_general | solution.py:70
  121.3 12.5 %fusion.12 = f32[2,8,12,3584]{3,2,1,0:T(8,128)} fusion(bf16[1,2,3584,1024]{3,2,1,0:T(8,128)(2,1)} %param.19, f32[8,2,12,1024]{3,2,0,1:T(8,128)} %fusion.112, f32[8,2,12,1024]{3,2,0,1:T(8,128)} %fusion.82), kind=kOutput, calls=%fused_computation.16 | convolution fusion | flops 1410465792 | bytes 19005440 | tf_op jit(solution)/shard_map/sejf,edf->sejd/dot_general | solution.py:77
  133.8 8.9 %fusion.167 = bf16[8,2,12,1024]{3,2,0,1:T(8,128)(2,1)} fusion(f32[8,2,12,1024]{3,2,0,1:T(8,128)} %fusion.112, bf16[1,2,3584,1024]{3,2,1,0:T(8,128)(2,1)} %param.19, bf16[8,2,12,3584]{3,2,1,0:T(8,128)(2,1)S(1)} %bitcast.297, f32[8,2,12,1024]{3,2,0,1:T(8,128)} %fusion.82), kind=kOutput, calls=%fused_computation.92 | convolution fusion | flops 1411252224 | bytes 18022400 | tf_op jit(solution)/shard_map/sejd,edf->sejf/dot_general | solution.py:67
  142.8 11.3 %fusion.56 = bf16[8,2,12,3584]{3,2,0,1:T(8,128)(2,1)S(1)} fusion(f32[2,8,12,3584]{3,2,1,0:T(8,128)} %fusion.12, bf16[8,2,12,1024]{3,2,0,1:T(8,128)(2,1)} %fusion.167, bf16[1,2,3584,1024]{3,2,1,0:T(8,128)(2,1)} %param.18), kind=kOutput, calls=%fused_computation.50 | convolution fusion | flops 1410662400 | bytes 19202048 | tf_op jit(solution)/shard_map/sejf,edf->sejd/dot_general | solution.py:75
  155.5 5.5 %all-to-all-start.6 = ((bf16[16,12,3584]{2,1,0:T(8,128)(2,1)}), bf16[16,12,3584]{2,1,0:T(8,128)(2,1)S(1)}, u32[]{:S(2)}, u32[]{:S(2)}) async-start(bf16[16,12,3584]{2,1,0:T(8,128)(2,1)} %bitcast.300), calls=%async_computation.6 | async-start | bytes 3670016 | tf_op jit(solution)/shard_map/all_to_all | solution.py:162
  161.0 7.9 %fusion.72 = f32[8,2,12,1024]{3,2,0,1:T(8,128)S(1)} fusion(bf16[1,2,3584,1024]{3,2,1,0:T(8,128)(2,1)} %param.18, bf16[8,2,12,3584]{3,2,1,0:T(8,128)(2,1)} %bitcast.3), kind=kOutput, calls=%fused_computation.73 | convolution fusion | flops 1409286144 | bytes 16842752 | tf_op jit(solution)/shard_map/sejd,edf->sejf/dot_general | solution.py:51
  169.0 8.2 %fusion.172 = bf16[8,2,12,1024]{3,2,0,1:T(8,128)(2,1)S(1)} fusion(bf16[1,2,3584,1024]{3,2,1,0:T(8,128)(2,1)} %param.19, bf16[8,2,12,3584]{3,2,1,0:T(8,128)(2,1)} %bitcast.3, f32[8,2,12,1024]{3,2,0,1:T(8,128)S(1)} %fusion.72), kind=kOutput, calls=%fused_computation.93 | convolution fusion | flops 1410465792 | bytes 17235968 | tf_op jit(solution)/shard_map/sejd,edf->sejf/dot_general | solution.py:52
  180.6 23.7 %all-to-all-done.6 = bf16[16,12,3584]{2,1,0:T(8,128)(2,1)S(1)} async-done(((bf16[16,12,3584]{2,1,0:T(8,128)(2,1)}), bf16[16,12,3584]{2,1,0:T(8,128)(2,1)S(1)}, u32[]{:S(2)}, u32[]{:S(2)}) %all-to-all-start.6) | async-done | bytes 1376288 | tf_op jit(solution)/shard_map/all_to_all | solution.py:162
  205.6 4.3 all-to-all-start.1
  226.7 26.7 %all-to-all-done.1 = bf16[16,12,3584]{2,1,0:T(8,128)(2,1)} async-done(((bf16[16,12,3584]{2,1,0:T(8,128)(2,1)}), bf16[16,12,3584]{2,1,0:T(8,128)(2,1)}, u32[]{:S(2)}, u32[]{:S(2)}) %all-to-all-start.1) | async-done | bytes 1376288 | tf_op jit(solution)/shard_map/all_to_all | solution.py:161
  285.5 14.9 %all-to-all-done.8 = bf16[16,12,3584]{2,1,0:T(8,128)(2,1)S(1)} async-done(((bf16[16,12,3584]{2,1,0:T(8,128)(2,1)}), bf16[16,12,3584]{2,1,0:T(8,128)(2,1)S(1)}, u32[]{:S(2)}, u32[]{:S(2)}) %all-to-all-start.8) | async-done | bytes 1376288 | tf_op jit(solution)/shard_map/all_to_all | solution.py:154
  300.4 4.3 all-to-all-start.7
  309.2 10.3 %collective-permute-done = bf16[64,3584]{1,0:T(8,128)(2,1)S(1)} collective-permute-done((bf16[64,3584]{1,0:T(8,128)(2,1)}, bf16[64,3584]{1,0:T(8,128)(2,1)S(1)}, u32[]{:S(2)}, u32[]{:S(2)}) %collective-permute-start) | collective-permute-done | bytes 458784 | tf_op jit(solution)/shard_map/ppermute | solution.py:19
  323.6 7.2 %fusion.87 = f32[8,2,12,1024]{3,2,0,1:T(8,128)S(1)} fusion(bf16[1,2,3584,1024]{3,2,1,0:T(8,128)(2,1)} %param.18, bf16[8,2,12,3584]{3,2,1,0:T(8,128)(2,1)S(1)} %bitcast.298), kind=kOutput, calls=%fused_computation.76 | convolution fusion | flops 1409286144 | bytes 16842752 | tf_op jit(solution)/shard_map/sejd,edf->sejf/dot_general | solution.py:66
  330.9 17.2 %all-to-all-done.7 = bf16[16,12,3584]{2,1,0:T(8,128)(2,1)} async-done(((bf16[16,12,3584]{2,1,0:T(8,128)(2,1)}), bf16[16,12,3584]{2,1,0:T(8,128)(2,1)}, u32[]{:S(2)}, u32[]{:S(2)}) %all-to-all-start.7) | async-done | bytes 1376288 | tf_op jit(solution)/shard_map/all_to_all | solution.py:155
  348.1 4.7 all-to-all-start.2
  352.9 11.4 %fusion.117 = f32[8,2,12,1024]{3,2,0,1:T(8,128)} fusion(bf16[1,2,1024,3584]{3,2,1,0:T(8,128)(2,1)} %param.20, bf16[8,2,12,3584]{3,2,1,0:T(8,128)(2,1)} %bitcast.45), kind=kOutput, calls=%fused_computation.82 | convolution fusion | flops 1409286144 | bytes 16842752 | tf_op jit(solution)/shard_map/sejd,efd->sejf/dot_general | solution.py:70
  364.3 12.2 %fusion.8 = f32[2,8,12,3584]{3,2,1,0:T(8,128)} fusion(bf16[1,2,3584,1024]{3,2,1,0:T(8,128)(2,1)} %param.19, f32[8,2,12,1024]{3,2,0,1:T(8,128)} %fusion.117, f32[8,2,12,1024]{3,2,0,1:T(8,128)S(1)} %fusion.87), kind=kOutput, calls=%fused_computation.12 | convolution fusion | flops 1410465792 | bytes 19005440 | tf_op jit(solution)/shard_map/sejf,edf->sejd/dot_general | solution.py:77
  376.5 8.6 %fusion.162 = bf16[8,2,12,1024]{3,2,0,1:T(8,128)(2,1)} fusion(f32[8,2,12,1024]{3,2,0,1:T(8,128)} %fusion.117, bf16[1,2,3584,1024]{3,2,1,0:T(8,128)(2,1)} %param.19, bf16[8,2,12,3584]{3,2,1,0:T(8,128)(2,1)S(1)} %bitcast.299, f32[8,2,12,1024]{3,2,0,1:T(8,128)S(1)} %fusion.87), kind=kOutput, calls=%fused_computation.91 | convolution fusion | flops 1411252224 | bytes 18022400 | tf_op jit(solution)/shard_map/sejd,edf->sejf/dot_general | solution.py:67
  385.1 11.3 %fusion.59 = bf16[8,2,12,3584]{3,2,0,1:T(8,128)(2,1)S(1)} fusion(f32[2,8,12,3584]{3,2,1,0:T(8,128)} %fusion.8, bf16[8,2,12,1024]{3,2,0,1:T(8,128)(2,1)} %fusion.162, bf16[1,2,3584,1024]{3,2,1,0:T(8,128)(2,1)} %param.18), kind=kOutput, calls=%fused_computation.51 | convolution fusion | flops 1410662400 | bytes 19202048 | tf_op jit(solution)/shard_map/sejf,edf->sejd/dot_general | solution.py:75
  397.8 5.2 %all-to-all-start.9 = ((bf16[16,12,3584]{2,1,0:T(8,128)(2,1)}), bf16[16,12,3584]{2,1,0:T(8,128)(2,1)S(1)}, u32[]{:S(2)}, u32[]{:S(2)}) async-start(bf16[16,12,3584]{2,1,0:T(8,128)(2,1)} %bitcast.301), calls=%async_computation.9 | async-start | bytes 3670016 | tf_op jit(solution)/shard_map/all_to_all | solution.py:162
  403.1 7.9 %fusion.77 = f32[8,2,12,1024]{3,2,0,1:T(8,128)S(1)} fusion(bf16[1,2,3584,1024]{3,2,1,0:T(8,128)(2,1)} %param.18, bf16[8,2,12,3584]{3,2,1,0:T(8,128)(2,1)} %bitcast.21), kind=kOutput, calls=%fused_computation.74 | convolution fusion | flops 1409286144 | bytes 16842752 | tf_op jit(solution)/shard_map/sejd,edf->sejf/dot_general | solution.py:51
  411.0 8.2 %fusion.177 = bf16[8,2,12,1024]{3,2,0,1:T(8,128)(2,1)S(1)} fusion(bf16[1,2,3584,1024]{3,2,1,0:T(8,128)(2,1)} %param.19, bf16[8,2,12,3584]{3,2,1,0:T(8,128)(2,1)} %bitcast.21, f32[8,2,12,1024]{3,2,0,1:T(8,128)S(1)} %fusion.77), kind=kOutput, calls=%fused_computation.94 | convolution fusion | flops 1410465792 | bytes 17235968 | tf_op jit(solution)/shard_map/sejd,edf->sejf/dot_general | solution.py:52
  422.7 23.7 %all-to-all-done.9 = bf16[16,12,3584]{2,1,0:T(8,128)(2,1)S(1)} async-done(((bf16[16,12,3584]{2,1,0:T(8,128)(2,1)}), bf16[16,12,3584]{2,1,0:T(8,128)(2,1)S(1)}, u32[]{:S(2)}, u32[]{:S(2)}) %all-to-all-start.9) | async-done | bytes 1376288 | tf_op jit(solution)/shard_map/all_to_all | solution.py:162
  447.7 4.5 all-to-all-start.3
  467.0 28.6 %all-to-all-done.3 = bf16[16,12,3584]{2,1,0:T(8,128)(2,1)} async-done(((bf16[16,12,3584]{2,1,0:T(8,128)(2,1)}), bf16[16,12,3584]{2,1,0:T(8,128)(2,1)}, u32[]{:S(2)}, u32[]{:S(2)}) %all-to-all-start.3) | async-done | bytes 1376288 | tf_op jit(solution)/shard_map/all_to_all | solution.py:161
  (195 shorter events, 127.4 us)
Async XLA Ops:
  0.6 4.7 copy-start.21
  0.6 4.5 copy-start
  0.7 4.8 copy-start.22
  7.6 6.5 %copy-start.23 = (f32[1,4,64,2]{2,3,1,0:T(2,128)S(1)}, f32[1,4,64,2]{2,3,1,0:T(2,128)}, u32[]{:S(2)}) copy-start(f32[1,4,64,2]{2,3,1,0:T(2,128)} %param.23) | copy-start | bytes 6148
  7.6 6.9 %copy-start.13 = (bf16[1,64,3584]{2,1,0:T(8,128)(2,1)S(1)}, bf16[1,64,3584]{2,1,0:T(8,128)(2,1)}, u32[]{:S(2)}) copy-start(bf16[1,64,3584]{2,1,0:T(8,128)(2,1)} %param.15) | copy-start | bytes 1376260
  7.6 49.9 %all-to-all-start.5 = ((bf16[16,12,3584]{2,1,0:T(8,128)(2,1)}), bf16[16,12,3584]{2,1,0:T(8,128)(2,1)S(1)}, u32[]{:S(2)}, u32[]{:S(2)}) async-start(bf16[16,12,3584]{2,1,0:T(8,128)(2,1)} %reshape.450), calls=%async_computation.5 | async-start | bytes 3670016 | tf_op jit(solution)/shard_map/all_to_all | solution.py:154
  57.5 47.8 %all-to-all-start.4 = ((bf16[16,12,3584]{2,1,0:T(8,128)(2,1)}), bf16[16,12,3584]{2,1,0:T(8,128)(2,1)}, u32[]{:S(2)}, u32[]{:S(2)}) async-start(bf16[16,12,3584]{2,1,0:T(8,128)(2,1)} %reshape.448), calls=%async_computation.4 | async-start | bytes 3670016 | tf_op jit(solution)/shard_map/all_to_all | solution.py:155
  105.2 50.2 %all-to-all-start = ((bf16[16,12,3584]{2,1,0:T(8,128)(2,1)}), bf16[16,12,3584]{2,1,0:T(8,128)(2,1)}, u32[]{:S(2)}, u32[]{:S(2)}) async-start(bf16[16,12,3584]{2,1,0:T(8,128)(2,1)} %reshape.440), calls=%async_computation | async-start | bytes 3670016 | tf_op jit(solution)/shard_map/all_to_all | solution.py:147
  155.5 48.9 %all-to-all-start.6 = ((bf16[16,12,3584]{2,1,0:T(8,128)(2,1)}), bf16[16,12,3584]{2,1,0:T(8,128)(2,1)S(1)}, u32[]{:S(2)}, u32[]{:S(2)}) async-start(bf16[16,12,3584]{2,1,0:T(8,128)(2,1)} %bitcast.300), calls=%async_computation.6 | async-start | bytes 3670016 | tf_op jit(solution)/shard_map/all_to_all | solution.py:162
  161.0 16.2 %slice-start = ((s8[14680064]{0:T(1024)(128)(4,1)}), s8[4194304]{0:T(1024)(128)(4,1)S(1)}, s32[]{:S(2)}) async-start(s8[14680064]{0:T(1024)(128)(4,1)} %bitcast.292), calls=%async_computation.10 | async-start | bytes 8388608
  161.0 16.2 %slice-start.1 = ((s8[14680064]{0:T(1024)(128)(4,1)}), s8[4194304]{0:T(1024)(128)(4,1)S(1)}, s32[]{:S(2)}) async-start(s8[14680064]{0:T(1024)(128)(4,1)} %bitcast.292), calls=%async_computation.11 | async-start | bytes 8388608
  168.9 8.2 %slice-start.2 = ((s8[14680064]{0:T(1024)(128)(4,1)}), s8[4194304]{0:T(1024)(128)(4,1)S(1)}, s32[]{:S(2)}) async-start(s8[14680064]{0:T(1024)(128)(4,1)} %bitcast.292), calls=%async_computation.12 | async-start | bytes 8388608
  169.0 8.2 %slice-start.3 = ((s8[14680064]{0:T(1024)(128)(4,1)}), s8[2097152]{0:T(1024)(128)(4,1)S(1)}, s32[]{:S(2)}) async-start(s8[14680064]{0:T(1024)(128)(4,1)} %bitcast.292), calls=%async_computation.13 | async-start | bytes 4194304
  205.6 47.8 %all-to-all-start.1 = ((bf16[16,12,3584]{2,1,0:T(8,128)(2,1)}), bf16[16,12,3584]{2,1,0:T(8,128)(2,1)}, u32[]{:S(2)}, u32[]{:S(2)}) async-start(bf16[16,12,3584]{2,1,0:T(8,128)(2,1)} %bitcast.16), calls=%async_computation.1 | async-start | bytes 3670016 | tf_op jit(solution)/shard_map/all_to_all | solution.py:161
  223.3 48.1 %collective-permute-start.1 = (bf16[64,3584]{1,0:T(8,128)(2,1)}, bf16[64,3584]{1,0:T(8,128)(2,1)}, u32[]{:S(2)}, u32[]{:S(2)}) collective-permute-start(bf16[64,3584]{1,0:T(8,128)(2,1)} %fusion.202), channel_id=1, source_target_pairs={{8,0},{16,8},{24,16},{9,1},{17,9},{25,17},{10,2},{18,10},{26,18},{... | collective-permute-start | bytes 1376264 | tf_op jit(solution)/shard_map/ppermute | solution.py:19
  253.4 47.0 %all-to-all-start.8 = ((bf16[16,12,3584]{2,1,0:T(8,128)(2,1)}), bf16[16,12,3584]{2,1,0:T(8,128)(2,1)S(1)}, u32[]{:S(2)}, u32[]{:S(2)}) async-start(bf16[16,12,3584]{2,1,0:T(8,128)(2,1)} %reshape.456), calls=%async_computation.8 | async-start | bytes 3670016 | tf_op jit(solution)/shard_map/all_to_all | solution.py:154
  271.3 33.3 %copy-start.4 = (f32[64,3584]{1,0:T(8,128)}, f32[64,3584]{1,0:T(8,128)S(1)}, u32[]{:S(2)}) copy-start(f32[64,3584]{1,0:T(8,128)S(1)} %multiply_reduce_fusion.1) | copy-start | bytes 2752516
  285.5 19.2 %copy-start.11 = (bf16[1,64,3584]{2,1,0:T(8,128)(2,1)S(1)}, bf16[1,64,3584]{2,1,0:T(8,128)(2,1)}, u32[]{:S(2)}) copy-start(bf16[1,64,3584]{2,1,0:T(8,128)(2,1)} %param.13) | copy-start | bytes 1376260
  300.4 47.8 %all-to-all-start.7 = ((bf16[16,12,3584]{2,1,0:T(8,128)(2,1)}), bf16[16,12,3584]{2,1,0:T(8,128)(2,1)}, u32[]{:S(2)}, u32[]{:S(2)}) async-start(bf16[16,12,3584]{2,1,0:T(8,128)(2,1)} %reshape.454), calls=%async_computation.7 | async-start | bytes 3670016 | tf_op jit(solution)/shard_map/all_to_all | solution.py:155
  305.6 14.0 %collective-permute-start = (bf16[64,3584]{1,0:T(8,128)(2,1)}, bf16[64,3584]{1,0:T(8,128)(2,1)S(1)}, u32[]{:S(2)}, u32[]{:S(2)}) collective-permute-start(bf16[64,3584]{1,0:T(8,128)(2,1)} %fusion.192), channel_id=1, source_target_pairs={{0,8},{8,16},{16,24},{1,9},{9,17},{17,25},{2,10},{10,18},{18,26},{... | collective-permute-start | bytes 1376264 | tf_op jit(solution)/shard_map/ppermute | solution.py:19
  348.1 49.7 %all-to-all-start.2 = ((bf16[16,12,3584]{2,1,0:T(8,128)(2,1)}), bf16[16,12,3584]{2,1,0:T(8,128)(2,1)}, u32[]{:S(2)}, u32[]{:S(2)}) async-start(bf16[16,12,3584]{2,1,0:T(8,128)(2,1)} %reshape.444), calls=%async_computation.2 | async-start | bytes 3670016 | tf_op jit(solution)/shard_map/all_to_all | solution.py:147
  397.8 48.6 %all-to-all-start.9 = ((bf16[16,12,3584]{2,1,0:T(8,128)(2,1)}), bf16[16,12,3584]{2,1,0:T(8,128)(2,1)S(1)}, u32[]{:S(2)}, u32[]{:S(2)}) async-start(bf16[16,12,3584]{2,1,0:T(8,128)(2,1)} %bitcast.301), calls=%async_computation.9 | async-start | bytes 3670016 | tf_op jit(solution)/shard_map/all_to_all | solution.py:162
  403.0 16.2 %slice-start.4 = ((s8[14680064]{0:T(1024)(128)(4,1)}), s8[4194304]{0:T(1024)(128)(4,1)S(1)}, s32[]{:S(2)}) async-start(s8[14680064]{0:T(1024)(128)(4,1)} %bitcast.294), calls=%async_computation.14 | async-start | bytes 8388608
  403.1 16.2 %slice-start.5 = ((s8[14680064]{0:T(1024)(128)(4,1)}), s8[4194304]{0:T(1024)(128)(4,1)S(1)}, s32[]{:S(2)}) async-start(s8[14680064]{0:T(1024)(128)(4,1)} %bitcast.294), calls=%async_computation.15 | async-start | bytes 8388608
  411.0 8.2 %slice-start.6 = ((s8[14680064]{0:T(1024)(128)(4,1)}), s8[4194304]{0:T(1024)(128)(4,1)S(1)}, s32[]{:S(2)}) async-start(s8[14680064]{0:T(1024)(128)(4,1)} %bitcast.294), calls=%async_computation.16 | async-start | bytes 8388608
  411.0 8.2 %slice-start.7 = ((s8[14680064]{0:T(1024)(128)(4,1)}), s8[2097152]{0:T(1024)(128)(4,1)S(1)}, s32[]{:S(2)}) async-start(s8[14680064]{0:T(1024)(128)(4,1)} %bitcast.294), calls=%async_computation.17 | async-start | bytes 4194304
  447.7 4.5 copy-start.5
  447.7 4.5 copy-start.12
  447.7 5.4 %copy-start.15 = (bf16[1,64,3584]{2,1,0:T(8,128)(2,1)S(1)}, bf16[1,64,3584]{2,1,0:T(8,128)(2,1)}, u32[]{:S(2)}) copy-start(bf16[1,64,3584]{2,1,0:T(8,128)(2,1)} %param.15) | copy-start | bytes 1376260
  447.7 47.9 %all-to-all-start.3 = ((bf16[16,12,3584]{2,1,0:T(8,128)(2,1)}), bf16[16,12,3584]{2,1,0:T(8,128)(2,1)}, u32[]{:S(2)}, u32[]{:S(2)}) async-start(bf16[16,12,3584]{2,1,0:T(8,128)(2,1)} %bitcast.28), calls=%async_computation.3 | async-start | bytes 3670016 | tf_op jit(solution)/shard_map/all_to_all | solution.py:161
  505.9 4.2 copy-start.17
  505.9 4.3 copy-start.7
  (13 other events, 24.3 us)
where the time goes:
time: 522 us; the launch traced here: 513 us
  waiting for transfers between devices  205 us (39%)
  matrix products  150 us (29%)
  local copies, waits for them, and re-layouts  68.6 us (13%)
  starting transfers between devices  52.3 us (10%)
  other arithmetic  36.3 us (7%)
    all_to_all x2, waiting for transfers between devices, local(): lax.all_to_all(ahead, 'expert', split_axis=0, concat_axis=0, tiled=True)  55.2 us
    all_to_all x2, waiting for transfers between devices, local(): lax.all_to_all(behind, 'expert', split_axis=0, concat_axis=0, tiled=True)  47.4 us
    all_to_all x2, waiting for transfers between devices, local(): lax.all_to_all(grad_send, 'expert', split_axis=0, concat_axis=0, tiled=True)  46.3 us
    all_to_all x2, waiting for transfers between devices, local(): lax.all_to_all(normed_send, 'expert', split_axis=0, concat_axis=0, tiled=...  45.6 us
    dot_general x2, matrix products, expert_backward(): jnp.einsum('sejf,edf->sejd', d_up, up_local, preferred_element_type=jnp.f...  24.7 us
    dot_general x2, matrix products, expert_backward(): jnp.einsum('sejd,efd->sejf', grad_blocks, down_local, preferred_element_t...  23 us
    dot_general x2, matrix products, expert_backward(): jnp.einsum('sejf,edf->sejd', d_gate, gate_local, preferred_element_type=j...  22.6 us
    dot_general x2, matrix products, expert_backward(): jnp.einsum('sejd,edf->sejf', blocks, up_local, preferred_element_type=jnp...  17.5 us
  transfers between devices with their start and end apart: 12, of which 9 were waited for; matrix products, arithmetic and copies ran while one was open for 44% of the time, Pallas kernels for 0%

commit v1 on v0

v1 whole, which is shorter than its diff:
```python
import jax
import jax.numpy as jnp
from jax import lax
from jax.sharding import PartitionSpec as P

EXPERTS = 16
TOPK = 2
TICKS = 2
CAP = 12


EPSILON = 1e-06
ROUTE_SCALE = 2.5


def passed_along(value, axis, steps):
    count = lax.axis_size(axis)
    leading, last = (max(0, -steps), min(count, count - steps))
    return lax.ppermute(value, axis, [(source, source + steps) for source in range(leading, last)])


def normalized(values, gain):
    floats = values.astype(jnp.float32)
    inverse = lax.rsqrt(jnp.mean(floats * floats, axis=-1, keepdims=True) + EPSILON)
    return (floats, inverse, (floats * inverse * gain).astype(jnp.bfloat16))


def gate_values(scores):
    return ROUTE_SCALE * scores / jnp.sum(scores, axis=-1, keepdims=True)


def slot_table(chosen_ids, capacity, experts, local_count, me):
    flat = chosen_ids.reshape(-1)
    onehot = (flat[:, None] == jnp.arange(experts, dtype=jnp.int32)[None, :]).astype(jnp.int32)
    earlier = jnp.cumsum(onehot, axis=0) - onehot
    place = jnp.sum(earlier * onehot, axis=1)
    block = jnp.bitwise_xor(flat // local_count, me)
    return block * (local_count * capacity) + (flat % local_count) * capacity + place


def slot_selector(slots, total_slots):
    return (slots[:, None] == jnp.arange(total_slots, dtype=jnp.int32)[None, :]).astype(
        jnp.bfloat16
    )


def exchanged(parts, groups):
    size = parts[0].shape[0] // groups
    received = [[part[:size] for part in parts]]
    for k in range(1, groups):
        block = jnp.concatenate([part[k * size : (k + 1) * size] for part in parts])
        landed = lax.ppermute(block, "expert", [(i, i ^ k) for i in range(groups)])
        received.append([landed[i * size : (i + 1) * size] for i in range(len(parts))])
    return [jnp.concatenate([blocks[i] for blocks in received]) for i in range(len(parts))]


def row_masks(total_slots, local_count):
    row = jnp.arange(total_slots, dtype=jnp.int32)
    owner = (row // CAP) % local_count
    return [(owner == e)[:, None] for e in range(local_count)]


def dot(a, b, dims):
    return lax.dot_general(a, b, (dims, ((), ())), preferred_element_type=jnp.float32)


def by_row(values, masks):
    total = values[0]
    for value, mask in zip(values[1:], masks[1:]):
        total = jnp.where(mask, value, total)
    return total


def spread(value, masks):
    return jnp.concatenate([jnp.where(m, value, jnp.zeros_like(value)) for m in masks], axis=1)


def expert_forward(x, gate_local, up_local, down_local, masks):
    count = gate_local.shape[0]
    pre_gate = by_row([dot(x, gate_local[e], ((1,), (0,))) for e in range(count)], masks)
    pre_up = by_row([dot(x, up_local[e], ((1,), (0,))) for e in range(count)], masks)
    active = (jax.nn.silu(pre_gate) * pre_up).astype(jnp.bfloat16)
    down = down_local.reshape(-1, down_local.shape[-1])
    return dot(spread(active, masks), down, ((1,), (0,))).astype(jnp.bfloat16)


def expert_backward(x, grad, gate_local, up_local, down_local, masks):
    count = gate_local.shape[0]
    pre_gate = by_row([dot(x, gate_local[e], ((1,), (0,))) for e in range(count)], masks)
    pre_up = by_row([dot(x, up_local[e], ((1,), (0,))) for e in range(count)], masks)
    sigma = jax.nn.sigmoid(pre_gate)
    swish = pre_gate * sigma
    down = down_local.reshape(-1, down_local.shape[-1])
    both = dot(grad, down, ((1,), (1,)))
    hidden = down_local.shape[1]
    act_grad = by_row([both[:, e * hidden : (e + 1) * hidden] for e in range(count)], masks)
    d_gate = (act_grad * pre_up * sigma * (1.0 + pre_gate * (1.0 - sigma))).astype(jnp.bfloat16)
    d_up = (act_grad * swish).astype(jnp.bfloat16)
    sums = [
        dot(d_gate, gate_local[e], ((1,), (1,))) + dot(d_up, up_local[e], ((1,), (1,)))
        for e in range(count)
    ]
    return by_row(sums, masks).astype(jnp.bfloat16)


def local(
    forward_held,
    forward_enter,
    backward_held,
    backward_enter,
    stashed_inputs,
    gate_weight,
    up_weight,
    down_weight,
    norm_gain,
    expert_ids,
    router_scores,
):
    position = lax.axis_index("section")
    sections = lax.axis_size("section")
    me = lax.axis_index("expert")
    groups = lax.axis_size("expert")
    weights = (gate_weight[0], up_weight[0], down_weight[0])
    local_count = weights[0].shape[0]
    gain = norm_gain[0]
    rows = forward_held.shape[1]
    total_slots = EXPERTS * CAP
    masks = row_masks(total_slots, local_count)

    selects = []
    gates = []
    for j in range(2 * TICKS):
        slots = slot_table(expert_ids[0, j], CAP, EXPERTS, local_count, me)
        selects.append(slot_selector(slots, total_slots).reshape(rows, TOPK, total_slots))
        gates.append(gate_values(router_scores[0, j]))

    def dispatched(select, values):
        return dot(jnp.sum(select, axis=1), values, ((0,), (0,)))

    behind = []
    for tick in range(TICKS):
        floats, inverse, normed = normalized(stashed_inputs[0, tick], gain)
        sent = dispatched(selects[TICKS + tick], normed).astype(jnp.bfloat16)
        behind.append((floats, inverse, sent))

    def ahead_start(layer_input, tick):
        normed = normalized(layer_input, gain)[2]
        return dispatched(selects[tick], normed).astype(jnp.bfloat16)

    def ahead_end(layer_input, returned, tick):
        select = selects[tick]
        branch = sum(
            gates[tick][:, k : k + 1] * dot(select[:, k], returned, ((1,), (0,)))
            for k in range(TOPK)
        )
        return (layer_input.astype(jnp.float32) + branch).astype(jnp.bfloat16)

    def behind_start(cotangent, tick):
        select = selects[TICKS + tick]
        slot_gates = jnp.sum(
            select.astype(jnp.float32) * gates[TICKS + tick][:, :, None], axis=(0, 1)
        )
        return (slot_gates[:, None] * dispatched(select, cotangent)).astype(jnp.bfloat16)

    def behind_end(cotangent, returned, tick):
        floats, inverse, _ = behind[tick]
        tokens = jnp.sum(selects[TICKS + tick], axis=1)
        combined = dot(tokens, returned, ((1,), (0,))) * gain
        norm_term = inverse * combined - floats * inverse**3 * jnp.mean(
            floats * combined, axis=-1, keepdims=True
        )
        return (cotangent.astype(jnp.float32) + norm_term).astype(jnp.bfloat16)

    layer_input = forward_held[0]
    cotangent = backward_held[0]
    forward_rows = []
    backward_rows = []
    (behind_normed,) = exchanged([behind[0][2]], groups)
    for tick in range(TICKS):
        (behind_grad,) = exchanged([behind_start(cotangent, tick)], groups)
        (ahead_normed,) = exchanged([ahead_start(layer_input, tick)], groups)
        behind_result = expert_backward(behind_normed, behind_grad, *weights, masks)
        (behind_back,) = exchanged([behind_result], groups)
        ahead_result = expert_forward(ahead_normed, *weights, masks)
        (ahead_back,) = exchanged([ahead_result], groups)
        returned = behind_end(cotangent, behind_back, tick)
        produced = ahead_end(layer_input, ahead_back, tick)
        forward_rows.append(produced)
        backward_rows.append(returned)
        if tick + 1 < TICKS:
            (behind_normed,) = exchanged([behind[tick + 1][2]], groups)
            forward_recv = passed_along(produced, "section", 1)
            backward_recv = passed_along(returned, "section", -1)
            layer_input = jnp.where(position == 0, forward_enter[tick], forward_recv)
            cotangent = jnp.where(position == sections - 1, backward_enter[tick], backward_recv)
    return (jnp.stack(forward_rows)[:, None], jnp.stack(backward_rows)[:, None])


def solution(mesh):
    placed = (
        P("section", "expert", None),
        P(None, "expert", None),
        P("section", "expert", None),
        P(None, "expert", None),
        P("section", None, "expert", None),
        P("section", "expert", None, None),
        P("section", "expert", None, None),
        P("section", "expert", None, None),
        P("section", None),
        P("section", None, "expert", None),
        P("section", None, "expert", None),
    )
    return jax.shard_map(
        local,
        mesh=mesh,
        in_specs=placed,
        out_specs=(P(None, "section", "expert", None), P(None, "section", "expert", None)),
        check_vma=False,
    )
```

time: 522 us -> 464 us (0.89)
  the two profiles are of different devices: /device:TPU:0 before, /device:TPU:11 now
where the time goes in v1:
time: 464 us; the launch traced here: 455 us
  waiting for transfers between devices  193 us (42%)
  matrix products  162 us (35%)
  starting transfers between devices  80.4 us (17%)
  other arithmetic  8.78 us (2%)
  local copies, waits for them, and re-layouts  7.93 us (2%)
    ppermute x70, waiting for transfers between devices, exchanged(): landed = lax.ppermute(block, 'expert', [(i, i ^ k) for i in range(groups)])  193 us
    dot_general x40, matrix products, dot(): lax.dot_general(a, b, (dims, ((), ())), preferred_element_type=jnp.float32)  162 us
    ppermute x70, starting transfers between devices, exchanged(): landed = lax.ppermute(block, 'expert', [(i, i ^ k) for i in range(groups)])  74.1 us
  transfers between devices with their start and end apart: 72, of which 32 were waited for; matrix products, arithmetic and copies ran while one was open for 28% of the time, Pallas kernels for 0%

profile of v1, /device:TPU:11, one launch (start us, length us, event | category | flops | bytes accessed | tf_op | source)
XLA Modules:
  0.0 454.8 jit_solution(2639138899356174828)
XLA Ops:
  20.4 5.5 %collective-permute-done.37 = bf16[24,3584]{1,0:T(8,128)(2,1)S(1)} collective-permute-done((bf16[24,3584]{1,0:T(8,128)(2,1)S(1)}, bf16[24,3584]{1,0:T(8,128)(2,1)S(1)}, u32[]{:S(2)}, u32[]{:S(2)}) %collective-permute-start.37) | collective-permute-done | bytes 172064 | tf_op jit(solution)/shard_map/ppermute | solution.py:52
  26.7 6.0 %collective-permute-done.38 = bf16[24,3584]{1,0:T(8,128)(2,1)S(1)} collective-permute-done((bf16[24,3584]{1,0:T(8,128)(2,1)S(1)}, bf16[24,3584]{1,0:T(8,128)(2,1)S(1)}, u32[]{:S(2)}, u32[]{:S(2)}) %collective-permute-start.38) | collective-permute-done | bytes 172064 | tf_op jit(solution)/shard_map/ppermute | solution.py:52
  34.1 7.7 %collective-permute-done.39 = bf16[24,3584]{1,0:T(8,128)(2,1)S(1)} collective-permute-done((bf16[24,3584]{1,0:T(8,128)(2,1)S(1)}, bf16[24,3584]{1,0:T(8,128)(2,1)S(1)}, u32[]{:S(2)}, u32[]{:S(2)}) %collective-permute-start.39) | collective-permute-done | bytes 172064 | tf_op jit(solution)/shard_map/ppermute | solution.py:52
  45.3 5.8 %collective-permute-done.40 = bf16[24,3584]{1,0:T(8,128)(2,1)S(1)} collective-permute-done((bf16[24,3584]{1,0:T(8,128)(2,1)S(1)}, bf16[24,3584]{1,0:T(8,128)(2,1)S(1)}, u32[]{:S(2)}, u32[]{:S(2)}) %collective-permute-start.40) | collective-permute-done | bytes 172064 | tf_op jit(solution)/shard_map/ppermute | solution.py:52
  52.9 7.0 %collective-permute-done.41 = bf16[24,3584]{1,0:T(8,128)(2,1)S(1)} collective-permute-done((bf16[24,3584]{1,0:T(8,128)(2,1)S(1)}, bf16[24,3584]{1,0:T(8,128)(2,1)S(1)}, u32[]{:S(2)}, u32[]{:S(2)}) %collective-permute-start.41) | collective-permute-done | bytes 172064 | tf_op jit(solution)/shard_map/ppermute | solution.py:52
  63.2 7.6 %collective-permute-done.42 = bf16[24,3584]{1,0:T(8,128)(2,1)S(1)} collective-permute-done((bf16[24,3584]{1,0:T(8,128)(2,1)S(1)}, bf16[24,3584]{1,0:T(8,128)(2,1)S(1)}, u32[]{:S(2)}, u32[]{:S(2)}) %collective-permute-start.42) | collective-permute-done | bytes 172064 | tf_op jit(solution)/shard_map/ppermute | solution.py:52
  70.9 6.2 %fusion.30 = f32[192,1024]{1,0:T(8,128)} fusion(bf16[192,3584]{1,0:T(8,128)(2,1)S(1)} %constant_dynamic-update-slice_fusion.35, bf16[1,2,3584,1024]{3,2,1,0:T(8,128)(2,1)} %param.16), kind=kOutput, calls=%fused_computation.30 | convolution fusion | flops 1409286144 | bytes 9502720 | tf_op jit(solution)/shard_map/dot_general | solution.py:64
  91.6 6.7 %collective-permute-done.35 = bf16[24,3584]{1,0:T(8,128)(2,1)S(1)} collective-permute-done((bf16[24,3584]{1,0:T(8,128)(2,1)S(1)}, bf16[24,3584]{1,0:T(8,128)(2,1)S(1)}, u32[]{:S(2)}, u32[]{:S(2)}) %collective-permute-start.35) | collective-permute-done | bytes 172064 | tf_op jit(solution)/shard_map/ppermute | solution.py:52
  98.3 11.3 %fusion.238 = f32[192,2048]{1,0:T(8,128)} fusion(bf16[192,3584]{1,0:T(8,128)(2,1)S(1)} %constant_dynamic-update-slice_fusion.28, bf16[2048,3584]{1,0:T(8,128)(2,1)} %bitcast.309), kind=kOutput, calls=%fused_computation.381 | convolution fusion | flops 2818572288 | bytes 17629184 | tf_op jit(solution)/shard_map/dot_general | solution.py:64
  109.6 5.9 %multiply_convert_fusion.1 = (bf16[192,1024]{1,0:T(8,128)(2,1)S(1)}, f32[192,1024]{1,0:T(8,128)S(1)}) fusion(f32[192,2048]{1,0:T(8,128)} %fusion.238, pred[192]{0:T(512)(128)(4,1)S(1)} %copy-done.23, f32[192,1024]{1,0:T(8,128)} %fusion.30, bf16[192,3584]{1,0:T(8,128)(2,1)S(1)} %copy-done.17, bf16[1,2,3584,1024]{3,2,1,0:T(8,128)(2,1)} %param.16), kind=kOutput, calls=%fused_computation.165 | convolution fusion | flops 1410859008 | bytes 12255424 | tf_op jit(solution)/shard_map/dot_general | solution.py:64
  115.6 5.8 %fusion.4 = f32[192,3584]{1,0:T(8,128)S(1)} fusion(bf16[192,1024]{1,0:T(8,128)(2,1)S(1)} %get-tuple-element.120, bf16[1,2,3584,1024]{3,2,1,0:T(8,128)(2,1)} %param.17), kind=kOutput, calls=%fused_computation.4 | convolution fusion | flops 1409286144 | bytes 10485760 | tf_op jit(solution)/shard_map/dot_general | solution.py:64
  121.4 7.3 %fusion.16 = f32[192,3584]{1,0:T(8,128)} fusion(bf16[192,1024]{1,0:T(8,128)(2,1)S(1)} %get-tuple-element.120, bf16[1,2,3584,1024]{3,2,1,0:T(8,128)(2,1)} %param.17), kind=kOutput, calls=%fused_computation.16 | convolution fusion | flops 1409286144 | bytes 10485760 | tf_op jit(solution)/shard_map/dot_general | solution.py:64
  130.7 12.0 %collective-permute-done.5 = bf16[24,3584]{1,0:T(8,128)(2,1)S(1)} collective-permute-done((bf16[24,3584]{1,0:T(8,128)(2,1)S(1)}, bf16[24,3584]{1,0:T(8,128)(2,1)S(1)}, u32[]{:S(2)}, u32[]{:S(2)}) %collective-permute-start.5) | collective-permute-done | bytes 172064 | tf_op jit(solution)/shard_map/ppermute | solution.py:52
  148.2 5.8 %fusion.10 = f32[192,1024]{1,0:T(8,128)} fusion(bf16[192,3584]{1,0:T(8,128)(2,1)S(1)} %constant_dynamic-update-slice_fusion, bf16[1,2,3584,1024]{3,2,1,0:T(8,128)(2,1)} %param.17), kind=kOutput, calls=%fused_computation.10 | convolution fusion | flops 1409286144 | bytes 9502720 | tf_op jit(solution)/shard_map/dot_general | solution.py:64
  161.7 5.7 %fusion.71 = bf16[192,3584]{1,0:T(8,128)(2,1)S(1)} fusion(bf16[192,3584]{1,0:T(8,128)(2,1)S(1)} %fusion.60, f32[192,3584]{1,0:T(8,128)S(1)} %copy-done.26, bf16[192,1024]{1,0:T(8,128)(2,1)S(1)} %fusion.135, bf16[1,2,3584,1024]{3,2,1,0:T(8,128)(2,1)} %param.16, pred[192]{0:T(512)(128)(4,1)S(1)} %copy-done.23), kind=kOutput, calls=%fused_computation.65 | convolution fusion | flops 1410662400 | bytes 13238464 | tf_op jit(solution)/shard_map/dot_general | solution.py:64
  182.8 8.3 %convolution_convert_fusion.4 = bf16[192,3584]{1,0:T(8,128)(2,1)S(1)} fusion(bf16[2048,3584]{1,0:T(8,128)(2,1)} %bitcast.310, bf16[192,1024]{1,0:T(8,128)(2,1)S(1)} %get-tuple-element.99, bf16[192,1024]{1,0:T(8,128)(2,1)S(1)} %get-tuple-element.98), kind=kOutput, calls=%fused_computation.62 | convolution fusion | flops 2820833280 | bytes 16842752 | tf_op jit(solution)/shard_map/dot_general | solution.py:64
  195.6 9.1 %collective-permute-done.48 = bf16[24,3584]{1,0:T(8,128)(2,1)S(1)} collective-permute-done((bf16[24,3584]{1,0:T(8,128)(2,1)S(1)}, bf16[24,3584]{1,0:T(8,128)(2,1)S(1)}, u32[]{:S(2)}, u32[]{:S(2)}) %collective-permute-start.48) | collective-permute-done | bytes 172064 | tf_op jit(solution)/shard_map/ppermute | solution.py:52
  212.9 11.8 %collective-permute-done.10 = bf16[24,3584]{1,0:T(8,128)(2,1)S(1)} collective-permute-done((bf16[24,3584]{1,0:T(8,128)(2,1)S(1)}, bf16[24,3584]{1,0:T(8,128)(2,1)S(1)}, u32[]{:S(2)}, u32[]{:S(2)}) %collective-permute-start.10) | collective-permute-done | bytes 172064 | tf_op jit(solution)/shard_map/ppermute | solution.py:52
  234.2 9.8 %collective-permute-done.13 = bf16[24,3584]{1,0:T(8,128)(2,1)S(1)} collective-permute-done((bf16[24,3584]{1,0:T(8,128)(2,1)S(1)}, bf16[24,3584]{1,0:T(8,128)(2,1)S(1)}, u32[]{:S(2)}, u32[]{:S(2)}) %collective-permute-start.13) | collective-permute-done | bytes 172064 | tf_op jit(solution)/shard_map/ppermute | solution.py:52
  251.5 7.6 %collective-permute-done.62 = bf16[24,3584]{1,0:T(8,128)(2,1)S(1)} collective-permute-done((bf16[24,3584]{1,0:T(8,128)(2,1)S(1)}, bf16[24,3584]{1,0:T(8,128)(2,1)S(1)}, u32[]{:S(2)}, u32[]{:S(2)}) %collective-permute-start.62) | collective-permute-done | bytes 172064 | tf_op jit(solution)/shard_map/ppermute | solution.py:52
  270.2 5.8 %fusion.2 = f32[192,1024]{1,0:T(8,128)} fusion(bf16[192,3584]{1,0:T(8,128)(2,1)S(1)} %constant_dynamic-update-slice_fusion.56, bf16[1,2,3584,1024]{3,2,1,0:T(8,128)(2,1)} %param.17), kind=kOutput, calls=%fused_computation.2 | convolution fusion | flops 1409286144 | bytes 9502720 | tf_op jit(solution)/shard_map/dot_general | solution.py:64
  294.9 9.0 %collective-permute-start.17 = (bf16[24,3584]{1,0:T(8,128)(2,1)S(1)}, bf16[24,3584]{1,0:T(8,128)(2,1)S(1)}, u32[]{:S(2)}, u32[]{:S(2)}) collective-permute-start(bf16[24,3584]{1,0:T(8,128)(2,1)S(1)} %get-tuple-element.76), channel_id=1, source_target_pairs={{0,3},{1,2},{2,1},{3,0},{4,7},{5,6},{6,5},{7,4},{8,11},{9,10},{10,... | collective-permute-start | bytes 516104 | tf_op jit(solution)/shard_map/ppermute | solution.py:52
  306.2 8.7 %collective-permute-done.57 = bf16[24,3584]{1,0:T(8,128)(2,1)S(1)} collective-permute-done((bf16[24,3584]{1,0:T(8,128)(2,1)S(1)}, bf16[24,3584]{1,0:T(8,128)(2,1)S(1)}, u32[]{:S(2)}, u32[]{:S(2)}) %collective-permute-start.57) | collective-permute-done | bytes 172064 | tf_op jit(solution)/shard_map/ppermute | solution.py:52
  314.8 11.2 %fusion.239 = f32[192,2048]{1,0:T(8,128)} fusion(bf16[192,3584]{1,0:T(8,128)(2,1)S(1)} %constant_dynamic-update-slice_fusion.49, bf16[2048,3584]{1,0:T(8,128)(2,1)} %bitcast.311), kind=kOutput, calls=%fused_computation.382 | convolution fusion | flops 2818572288 | bytes 17629184 | tf_op jit(solution)/shard_map/dot_general | solution.py:64
  326.0 5.7 %multiply_convert_fusion = (bf16[192,1024]{1,0:T(8,128)(2,1)S(1)}, f32[192,1024]{1,0:T(8,128)S(1)}) fusion(f32[192,2048]{1,0:T(8,128)} %fusion.239, pred[192]{0:T(512)(128)(4,1)S(1)} %copy-done.23, f32[192,1024]{1,0:T(8,128)} %fusion.26, bf16[192,3584]{1,0:T(8,128)(2,1)S(1)} %constant_dynamic-update-slice_fusion.56, bf16[1,2,3584,1024]{3,2,1,0:T(8,128)(2,1)} %param.16), kind=kOutput, calls=%fused_computation.163 | convolution fusion | flops 1410859008 | bytes 12255424 | tf_op jit(solution)/shard_map/dot_general | solution.py:64
  331.8 7.4 %fusion = f32[192,3584]{1,0:T(8,128)} fusion(bf16[192,1024]{1,0:T(8,128)(2,1)S(1)} %get-tuple-element.123, bf16[1,2,3584,1024]{3,2,1,0:T(8,128)(2,1)} %param.17), kind=kOutput, calls=%fused_computation | convolution fusion | flops 1409286144 | bytes 10485760 | tf_op jit(solution)/shard_map/dot_general | solution.py:64
  339.1 7.5 %fusion.12 = f32[192,3584]{1,0:T(8,128)} fusion(bf16[192,1024]{1,0:T(8,128)(2,1)S(1)} %get-tuple-element.123, bf16[1,2,3584,1024]{3,2,1,0:T(8,128)(2,1)} %param.17), kind=kOutput, calls=%fused_computation.12 | convolution fusion | flops 1409286144 | bytes 10485760 | tf_op jit(solution)/shard_map/dot_general | solution.py:64
  347.3 12.8 %collective-permute-done.20 = bf16[24,3584]{1,0:T(8,128)(2,1)S(1)} collective-permute-done((bf16[24,3584]{1,0:T(8,128)(2,1)S(1)}, bf16[24,3584]{1,0:T(8,128)(2,1)S(1)}, u32[]{:S(2)}, u32[]{:S(2)}) %collective-permute-start.20) | collective-permute-done | bytes 172064 | tf_op jit(solution)/shard_map/ppermute | solution.py:52
  365.3 5.8 %fusion.8 = f32[192,1024]{1,0:T(8,128)} fusion(bf16[192,3584]{1,0:T(8,128)(2,1)S(1)} %constant_dynamic-update-slice_fusion.14, bf16[1,2,3584,1024]{3,2,1,0:T(8,128)(2,1)} %param.17), kind=kOutput, calls=%fused_computation.8 | convolution fusion | flops 1409286144 | bytes 9502720 | tf_op jit(solution)/shard_map/dot_general | solution.py:64
  397.3 8.5 %convolution_convert_fusion.2 = bf16[192,3584]{1,0:T(8,128)(2,1)S(1)} fusion(bf16[2048,3584]{1,0:T(8,128)(2,1)} %bitcast.312, bf16[192,1024]{1,0:T(8,128)(2,1)S(1)} %get-tuple-element.97, bf16[192,1024]{1,0:T(8,128)(2,1)S(1)} %get-tuple-element.96), kind=kOutput, calls=%fused_computation.60 | convolution fusion | flops 2820833280 | bytes 16842752 | tf_op jit(solution)/shard_map/dot_general | solution.py:64
  410.2 9.1 %collective-permute-done.70 = bf16[24,3584]{1,0:T(8,128)(2,1)S(1)} collective-permute-done((bf16[24,3584]{1,0:T(8,128)(2,1)S(1)}, bf16[24,3584]{1,0:T(8,128)(2,1)S(1)}, u32[]{:S(2)}, u32[]{:S(2)}) %collective-permute-start.70) | collective-permute-done | bytes 172064 | tf_op jit(solution)/shard_map/ppermute | solution.py:52
  427.0 13.1 %collective-permute-done.25 = bf16[24,3584]{1,0:T(8,128)(2,1)S(1)} collective-permute-done((bf16[24,3584]{1,0:T(8,128)(2,1)S(1)}, bf16[24,3584]{1,0:T(8,128)(2,1)S(1)}, u32[]{:S(2)}, u32[]{:S(2)}) %collective-permute-start.25) | collective-permute-done | bytes 172064 | tf_op jit(solution)/shard_map/ppermute | solution.py:52
  (384 shorter events, 194.6 us)
Async XLA Ops:
  6.9 72.8 %collective-permute-start.29 = (bf16[24,3584]{1,0:T(8,128)(2,1)}, bf16[24,3584]{1,0:T(8,128)(2,1)S(1)}, u32[]{:S(2)}, u32[]{:S(2)}) collective-permute-start(bf16[24,3584]{1,0:T(8,128)(2,1)} %get-tuple-element.54), channel_id=1, source_target_pairs={{0,1},{1,0},{2,3},{3,2},{4,5},{5,4},{6,7},{7,6},{8,9},{9,8},{10,11... | collective-permute-start | bytes 516104 | tf_op jit(solution)/shard_map/ppermute | solution.py:52
  7.6 73.8 %collective-permute-start.30 = (bf16[24,3584]{1,0:T(8,128)(2,1)}, bf16[24,3584]{1,0:T(8,128)(2,1)S(1)}, u32[]{:S(2)}, u32[]{:S(2)}) collective-permute-start(bf16[24,3584]{1,0:T(8,128)(2,1)} %get-tuple-element.53), channel_id=1, source_target_pairs={{0,2},{1,3},{2,0},{3,1},{4,6},{5,7},{6,4},{7,5},{8,10},{9,11},{10,... | collective-permute-start | bytes 516104 | tf_op jit(solution)/shard_map/ppermute | solution.py:52
  7.8 74.3 %collective-permute-start.31 = (bf16[24,3584]{1,0:T(8,128)(2,1)}, bf16[24,3584]{1,0:T(8,128)(2,1)S(1)}, u32[]{:S(2)}, u32[]{:S(2)}) collective-permute-start(bf16[24,3584]{1,0:T(8,128)(2,1)} %get-tuple-element.52), channel_id=1, source_target_pairs={{0,3},{1,2},{2,1},{3,0},{4,7},{5,6},{6,5},{7,4},{8,11},{9,10},{10,... | collective-permute-start | bytes 516104 | tf_op jit(solution)/shard_map/ppermute | solution.py:52
  9.2 73.4 %collective-permute-start.32 = (bf16[24,3584]{1,0:T(8,128)(2,1)S(1)}, bf16[24,3584]{1,0:T(8,128)(2,1)S(1)}, u32[]{:S(2)}, u32[]{:S(2)}) collective-permute-start(bf16[24,3584]{1,0:T(8,128)(2,1)S(1)} %get-tuple-element.51), channel_id=1, source_target_pairs={{0,4},{1,5},{2,6},{3,7},{4,0},{5,1},{6,2},{7,3},{8,12},{9,13},{10,... | collective-permute-start | bytes 516104 | tf_op jit(solution)/shard_map/ppermute | solution.py:52
  82.1 46.6 %collective-permute-start = (bf16[24,3584]{1,0:T(8,128)(2,1)S(1)}, bf16[24,3584]{1,0:T(8,128)(2,1)S(1)}, u32[]{:S(2)}, u32[]{:S(2)}) collective-permute-start(bf16[24,3584]{1,0:T(8,128)(2,1)S(1)} %get-tuple-element.94), channel_id=1, source_target_pairs={{0,1},{1,0},{2,3},{3,2},{4,5},{5,4},{6,7},{7,6},{8,9},{9,8},{10,11... | collective-permute-start | bytes 516104 | tf_op jit(solution)/shard_map/ppermute | solution.py:52
  82.6 47.9 %collective-permute-start.1 = (bf16[24,3584]{1,0:T(8,128)(2,1)S(1)}, bf16[24,3584]{1,0:T(8,128)(2,1)S(1)}, u32[]{:S(2)}, u32[]{:S(2)}) collective-permute-start(bf16[24,3584]{1,0:T(8,128)(2,1)S(1)} %get-tuple-element.93), channel_id=1, source_target_pairs={{0,2},{1,3},{2,0},{3,1},{4,6},{5,7},{6,4},{7,5},{8,10},{9,11},{10,... | collective-permute-start | bytes 516104 | tf_op jit(solution)/shard_map/ppermute | solution.py:52
  87.1 43.5 %collective-permute-start.2 = (bf16[24,3584]{1,0:T(8,128)(2,1)S(1)}, bf16[24,3584]{1,0:T(8,128)(2,1)S(1)}, u32[]{:S(2)}, u32[]{:S(2)}) collective-permute-start(bf16[24,3584]{1,0:T(8,128)(2,1)S(1)} %get-tuple-element.92), channel_id=1, source_target_pairs={{0,3},{1,2},{2,1},{3,0},{4,7},{5,6},{6,5},{7,4},{8,11},{9,10},{10,... | collective-permute-start | bytes 516104 | tf_op jit(solution)/shard_map/ppermute | solution.py:52
  91.5 39.1 %collective-permute-start.3 = (bf16[24,3584]{1,0:T(8,128)(2,1)S(1)}, bf16[24,3584]{1,0:T(8,128)(2,1)S(1)}, u32[]{:S(2)}, u32[]{:S(2)}) collective-permute-start(bf16[24,3584]{1,0:T(8,128)(2,1)S(1)} %get-tuple-element.91), channel_id=1, source_target_pairs={{0,4},{1,5},{2,6},{3,7},{4,0},{5,1},{6,2},{7,3},{8,12},{9,13},{10,... | collective-permute-start | bytes 516104 | tf_op jit(solution)/shard_map/ppermute | solution.py:52
  98.2 32.4 %collective-permute-start.4 = (bf16[24,3584]{1,0:T(8,128)(2,1)S(1)}, bf16[24,3584]{1,0:T(8,128)(2,1)S(1)}, u32[]{:S(2)}, u32[]{:S(2)}) collective-permute-start(bf16[24,3584]{1,0:T(8,128)(2,1)S(1)} %get-tuple-element.90), channel_id=1, source_target_pairs={{0,5},{1,4},{2,7},{3,6},{4,1},{5,0},{6,3},{7,2},{8,13},{9,12},{10,... | collective-permute-start | bytes 516104 | tf_op jit(solution)/shard_map/ppermute | solution.py:52
  168.0 23.3 %collective-permute-start.43 = (bf16[24,3584]{1,0:T(8,128)(2,1)S(1)}, bf16[24,3584]{1,0:T(8,128)(2,1)S(1)}, u32[]{:S(2)}, u32[]{:S(2)}) collective-permute-start(bf16[24,3584]{1,0:T(8,128)(2,1)S(1)} %get-tuple-element.46), channel_id=1, source_target_pairs={{0,1},{1,0},{2,3},{3,2},{4,5},{5,4},{6,7},{7,6},{8,9},{9,8},{10,11... | collective-permute-start | bytes 516104 | tf_op jit(solution)/shard_map/ppermute | solution.py:52
  168.4 23.0 %collective-permute-start.44 = (bf16[24,3584]{1,0:T(8,128)(2,1)S(1)}, bf16[24,3584]{1,0:T(8,128)(2,1)S(1)}, u32[]{:S(2)}, u32[]{:S(2)}) collective-permute-start(bf16[24,3584]{1,0:T(8,128)(2,1)S(1)} %get-tuple-element.45), channel_id=1, source_target_pairs={{0,2},{1,3},{2,0},{3,1},{4,6},{5,7},{6,4},{7,5},{8,10},{9,11},{10,... | collective-permute-start | bytes 516104 | tf_op jit(solution)/shard_map/ppermute | solution.py:52
  168.4 24.8 %collective-permute-start.45 = (bf16[24,3584]{1,0:T(8,128)(2,1)S(1)}, bf16[24,3584]{1,0:T(8,128)(2,1)S(1)}, u32[]{:S(2)}, u32[]{:S(2)}) collective-permute-start(bf16[24,3584]{1,0:T(8,128)(2,1)S(1)} %get-tuple-element.44), channel_id=1, source_target_pairs={{0,3},{1,2},{2,1},{3,0},{4,7},{5,6},{6,5},{7,4},{8,11},{9,10},{10,... | collective-permute-start | bytes 516104 | tf_op jit(solution)/shard_map/ppermute | solution.py:52
  170.2 23.3 %collective-permute-start.46 = (bf16[24,3584]{1,0:T(8,128)(2,1)S(1)}, bf16[24,3584]{1,0:T(8,128)(2,1)S(1)}, u32[]{:S(2)}, u32[]{:S(2)}) collective-permute-start(bf16[24,3584]{1,0:T(8,128)(2,1)S(1)} %get-tuple-element.43), channel_id=1, source_target_pairs={{0,4},{1,5},{2,6},{3,7},{4,0},{5,1},{6,2},{7,3},{8,12},{9,13},{10,... | collective-permute-start | bytes 516104 | tf_op jit(solution)/shard_map/ppermute | solution.py:52
  170.2 25.1 %collective-permute-start.47 = (bf16[24,3584]{1,0:T(8,128)(2,1)S(1)}, bf16[24,3584]{1,0:T(8,128)(2,1)S(1)}, u32[]{:S(2)}, u32[]{:S(2)}) collective-permute-start(bf16[24,3584]{1,0:T(8,128)(2,1)S(1)} %get-tuple-element.42), channel_id=1, source_target_pairs={{0,5},{1,4},{2,7},{3,6},{4,1},{5,0},{6,3},{7,2},{8,13},{9,12},{10,... | collective-permute-start | bytes 516104 | tf_op jit(solution)/shard_map/ppermute | solution.py:52
  210.7 23.4 %collective-permute-start.12 = (bf16[24,3584]{1,0:T(8,128)(2,1)S(1)}, bf16[24,3584]{1,0:T(8,128)(2,1)S(1)}, u32[]{:S(2)}, u32[]{:S(2)}) collective-permute-start(bf16[24,3584]{1,0:T(8,128)(2,1)S(1)} %get-tuple-element.81), channel_id=1, source_target_pairs={{0,6},{1,7},{2,4},{3,5},{4,2},{5,3},{6,0},{7,1},{8,14},{9,15},{10,... | collective-permute-start | bytes 516104 | tf_op jit(solution)/shard_map/ppermute | solution.py:52
  211.2 32.8 %collective-permute-start.13 = (bf16[24,3584]{1,0:T(8,128)(2,1)S(1)}, bf16[24,3584]{1,0:T(8,128)(2,1)S(1)}, u32[]{:S(2)}, u32[]{:S(2)}) collective-permute-start(bf16[24,3584]{1,0:T(8,128)(2,1)S(1)} %get-tuple-element.80), channel_id=1, source_target_pairs={{0,7},{1,6},{2,5},{3,4},{4,3},{5,2},{6,1},{7,0},{8,15},{9,14},{10,... | collective-permute-start | bytes 516104 | tf_op jit(solution)/shard_map/ppermute | solution.py:52
  212.2 32.6 %collective-permute-start.58 = (bf16[24,3584]{1,0:T(8,128)(2,1)S(1)}, bf16[24,3584]{1,0:T(8,128)(2,1)S(1)}, u32[]{:S(2)}, u32[]{:S(2)}) collective-permute-start(bf16[24,3584]{1,0:T(8,128)(2,1)S(1)} %get-tuple-element.38), channel_id=1, source_target_pairs={{0,1},{1,0},{2,3},{3,2},{4,5},{5,4},{6,7},{7,6},{8,9},{9,8},{10,11... | collective-permute-start | bytes 516104 | tf_op jit(solution)/shard_map/ppermute | solution.py:52
  244.9 22.6 %collective-permute-start.64 = (bf16[24,3584]{1,0:T(8,128)(2,1)S(1)}, bf16[24,3584]{1,0:T(8,128)(2,1)S(1)}, u32[]{:S(2)}, u32[]{:S(2)}) collective-permute-start(bf16[24,3584]{1,0:T(8,128)(2,1)S(1)} %get-tuple-element.32), channel_id=1, source_target_pairs={{0,7},{1,6},{2,5},{3,4},{4,3},{5,2},{6,1},{7,0},{8,15},{9,14},{10,... | collective-permute-start | bytes 516104 | tf_op jit(solution)/shard_map/ppermute | solution.py:52
  245.0 30.9 %collective-permute-start.50 = (bf16[64,3584]{1,0:T(8,128)(2,1)S(1)}, bf16[64,3584]{1,0:T(8,128)(2,1)S(1)}, u32[]{:S(2)}, u32[]{:S(2)}) collective-permute-start(bf16[64,3584]{1,0:T(8,128)(2,1)S(1)} %fusion.165), channel_id=1, source_target_pairs={{8,0},{16,8},{24,16},{9,1},{17,9},{25,17},{10,2},{18,10},{26,18},{... | collective-permute-start | bytes 1376264 | tf_op jit(solution)/shard_map/ppermute | solution.py:19
  247.2 31.6 %collective-permute-start.14 = (bf16[64,3584]{1,0:T(8,128)(2,1)S(1)}, bf16[64,3584]{1,0:T(8,128)(2,1)S(1)}, u32[]{:S(2)}, u32[]{:S(2)}) collective-permute-start(bf16[64,3584]{1,0:T(8,128)(2,1)S(1)} %fusion.78), channel_id=1, source_target_pairs={{0,8},{8,16},{16,24},{1,9},{9,17},{17,25},{2,10},{10,18},{18,26},{... | collective-permute-start | bytes 1376264 | tf_op jit(solution)/shard_map/ppermute | solution.py:19
  282.3 23.8 %collective-permute-start.56 = (bf16[24,3584]{1,0:T(8,128)(2,1)S(1)}, bf16[24,3584]{1,0:T(8,128)(2,1)S(1)}, u32[]{:S(2)}, u32[]{:S(2)}) collective-permute-start(bf16[24,3584]{1,0:T(8,128)(2,1)S(1)} %get-tuple-element.25), channel_id=1, source_target_pairs={{0,6},{1,7},{2,4},{3,5},{4,2},{5,3},{6,0},{7,1},{8,14},{9,15},{10,... | collective-permute-start | bytes 516104 | tf_op jit(solution)/shard_map/ppermute | solution.py:52
  286.7 28.1 %collective-permute-start.57 = (bf16[24,3584]{1,0:T(8,128)(2,1)S(1)}, bf16[24,3584]{1,0:T(8,128)(2,1)S(1)}, u32[]{:S(2)}, u32[]{:S(2)}) collective-permute-start(bf16[24,3584]{1,0:T(8,128)(2,1)S(1)} %get-tuple-element.24), channel_id=1, source_target_pairs={{0,7},{1,6},{2,5},{3,4},{4,3},{5,2},{6,1},{7,0},{8,15},{9,14},{10,... | collective-permute-start | bytes 516104 | tf_op jit(solution)/shard_map/ppermute | solution.py:52
  290.7 55.9 %collective-permute-start.15 = (bf16[24,3584]{1,0:T(8,128)(2,1)S(1)}, bf16[24,3584]{1,0:T(8,128)(2,1)S(1)}, u32[]{:S(2)}, u32[]{:S(2)}) collective-permute-start(bf16[24,3584]{1,0:T(8,128)(2,1)S(1)} %get-tuple-element.78), channel_id=1, source_target_pairs={{0,1},{1,0},{2,3},{3,2},{4,5},{5,4},{6,7},{7,6},{8,9},{9,8},{10,11... | collective-permute-start | bytes 516104 | tf_op jit(solution)/shard_map/ppermute | solution.py:52
  291.5 55.5 %collective-permute-start.16 = (bf16[24,3584]{1,0:T(8,128)(2,1)S(1)}, bf16[24,3584]{1,0:T(8,128)(2,1)S(1)}, u32[]{:S(2)}, u32[]{:S(2)}) collective-permute-start(bf16[24,3584]{1,0:T(8,128)(2,1)S(1)} %get-tuple-element.77), channel_id=1, source_target_pairs={{0,2},{1,3},{2,0},{3,1},{4,6},{5,7},{6,4},{7,5},{8,10},{9,11},{10,... | collective-permute-start | bytes 516104 | tf_op jit(solution)/shard_map/ppermute | solution.py:52
  294.9 52.3 %collective-permute-start.17 = (bf16[24,3584]{1,0:T(8,128)(2,1)S(1)}, bf16[24,3584]{1,0:T(8,128)(2,1)S(1)}, u32[]{:S(2)}, u32[]{:S(2)}) collective-permute-start(bf16[24,3584]{1,0:T(8,128)(2,1)S(1)} %get-tuple-element.76), channel_id=1, source_target_pairs={{0,3},{1,2},{2,1},{3,0},{4,7},{5,6},{6,5},{7,4},{8,11},{9,10},{10,... | collective-permute-start | bytes 516104 | tf_op jit(solution)/shard_map/ppermute | solution.py:52
  306.1 41.1 %collective-permute-start.18 = (bf16[24,3584]{1,0:T(8,128)(2,1)S(1)}, bf16[24,3584]{1,0:T(8,128)(2,1)S(1)}, u32[]{:S(2)}, u32[]{:S(2)}) collective-permute-start(bf16[24,3584]{1,0:T(8,128)(2,1)S(1)} %get-tuple-element.75), channel_id=1, source_target_pairs={{0,4},{1,5},{2,6},{3,7},{4,0},{5,1},{6,2},{7,3},{8,12},{9,13},{10,... | collective-permute-start | bytes 516104 | tf_op jit(solution)/shard_map/ppermute | solution.py:52
  314.8 32.4 %collective-permute-start.19 = (bf16[24,3584]{1,0:T(8,128)(2,1)S(1)}, bf16[24,3584]{1,0:T(8,128)(2,1)S(1)}, u32[]{:S(2)}, u32[]{:S(2)}) collective-permute-start(bf16[24,3584]{1,0:T(8,128)(2,1)S(1)} %get-tuple-element.74), channel_id=1, source_target_pairs={{0,5},{1,4},{2,7},{3,6},{4,1},{5,0},{6,3},{7,2},{8,13},{9,12},{10,... | collective-permute-start | bytes 516104 | tf_op jit(solution)/shard_map/ppermute | solution.py:52
  385.1 20.8 %collective-permute-start.65 = (bf16[24,3584]{1,0:T(8,128)(2,1)S(1)}, bf16[24,3584]{1,0:T(8,128)(2,1)S(1)}, u32[]{:S(2)}, u32[]{:S(2)}) collective-permute-start(bf16[24,3584]{1,0:T(8,128)(2,1)S(1)} %get-tuple-element.22), channel_id=1, source_target_pairs={{0,1},{1,0},{2,3},{3,2},{4,5},{5,4},{6,7},{7,6},{8,9},{9,8},{10,11... | collective-permute-start | bytes 516104 | tf_op jit(solution)/shard_map/ppermute | solution.py:52
  386.3 21.5 %collective-permute-start.67 = (bf16[24,3584]{1,0:T(8,128)(2,1)S(1)}, bf16[24,3584]{1,0:T(8,128)(2,1)S(1)}, u32[]{:S(2)}, u32[]{:S(2)}) collective-permute-start(bf16[24,3584]{1,0:T(8,128)(2,1)S(1)} %get-tuple-element.20), channel_id=1, source_target_pairs={{0,3},{1,2},{2,1},{3,0},{4,7},{5,6},{6,5},{7,4},{8,11},{9,10},{10,... | collective-permute-start | bytes 516104 | tf_op jit(solution)/shard_map/ppermute | solution.py:52
  388.4 21.5 %collective-permute-start.69 = (bf16[24,3584]{1,0:T(8,128)(2,1)S(1)}, bf16[24,3584]{1,0:T(8,128)(2,1)S(1)}, u32[]{:S(2)}, u32[]{:S(2)}) collective-permute-start(bf16[24,3584]{1,0:T(8,128)(2,1)S(1)} %get-tuple-element.18), channel_id=1, source_target_pairs={{0,5},{1,4},{2,7},{3,6},{4,1},{5,0},{6,3},{7,2},{8,13},{9,12},{10,... | collective-permute-start | bytes 516104 | tf_op jit(solution)/shard_map/ppermute | solution.py:52
  425.5 23.3 %collective-permute-start.27 = (bf16[24,3584]{1,0:T(8,128)(2,1)S(1)}, bf16[24,3584]{1,0:T(8,128)(2,1)S(1)}, u32[]{:S(2)}, u32[]{:S(2)}) collective-permute-start(bf16[24,3584]{1,0:T(8,128)(2,1)S(1)} %get-tuple-element.65), channel_id=1, source_target_pairs={{0,6},{1,7},{2,4},{3,5},{4,2},{5,3},{6,0},{7,1},{8,14},{9,15},{10,... | collective-permute-start | bytes 516104 | tf_op jit(solution)/shard_map/ppermute | solution.py:52
  426.6 26.0 %collective-permute-start.28 = (bf16[24,3584]{1,0:T(8,128)(2,1)S(1)}, bf16[24,3584]{1,0:T(8,128)(2,1)S(1)}, u32[]{:S(2)}, u32[]{:S(2)}) collective-permute-start(bf16[24,3584]{1,0:T(8,128)(2,1)S(1)} %get-tuple-element.64), channel_id=1, source_target_pairs={{0,7},{1,6},{2,5},{3,4},{4,3},{5,2},{6,1},{7,0},{8,15},{9,14},{10,... | collective-permute-start | bytes 516104 | tf_op jit(solution)/shard_map/ppermute | solution.py:52
  (86 other events, 1501.0 us)
